TPU v7x, 256 devices: a whole 4x4x8 slice. The times are simulated.
256 devices in a mesh: row: 16 (over z, core), col: 16 (over y, x).
Axes of the slice: x: 4, y: 4, z: 8, core: 2. Of those that a mesh axis runs over, the one named last changes fastest.
Arguments:
- momentum: float32 [8192, 26624], P('row', 'col'), may hold values from -20 to 20
- grad: bfloat16 [8192, 26624], P('row', 'col'), may hold values from -3 to 3
- basis: float32 [26624, 128], P('col'), may hold values from -0.0390625 to 0.0390625
Outputs:
- momentum_out: float32 [8192, 26624], P('row', 'col')
- left_out: float32 [2, 8192, 128], P(None, 'row')
- right_out: float32 [26624, 128], P('col')
All inputs are finite; a program needn't handle non-finite values.
Results may differ from a plain program's by a relative error of at most 0.0003.
Values sent between devices are 32-bit elements; how exact they have to be, the bound alone decides.
A program may use at most 64 MiB of HBM per device.

v0:
```python
import jax
import jax.numpy as jnp
from jax import lax
from jax.sharding import PartitionSpec as P

ITERS = 2


def chol_solve(share, gram):
    lower = jnp.linalg.cholesky(gram)
    return jax.scipy.linalg.solve_triangular(lower, share.T, lower=True).T


def gram_of(share):
    return lax.dot_general(share, share, (((0,), (0,)), ((), ())), precision=lax.Precision.HIGHEST)


def shards(momentum, grad, basis):
    work = momentum + grad.astype(jnp.float32)
    row_count = momentum.shape[0]
    col_count = momentum.shape[1]
    total_rows = row_count * lax.axis_size("row")
    total_cols = col_count * lax.axis_size("col")
    lefts = []
    for step in range(ITERS):
        current = work
        current_basis = basis
        proj = lax.psum(jnp.dot(current, current_basis, precision=lax.Precision.HIGHEST), "col")
        gram_left = lax.psum(gram_of(proj), "row")
        left = chol_solve(proj, gram_left)
        partial_right = lax.dot_general(
            current, left, (((0,), (0,)), ((), ())), precision=lax.Precision.HIGHEST
        )
        right_raw = lax.psum(partial_right, "row")
        gram_right = lax.psum(gram_of(right_raw), "col")
        basis = chol_solve(right_raw, gram_right)
        outer = lax.dot_general(
            left, right_raw, (((1,), (1,)), ((), ())), precision=lax.Precision.HIGHEST
        )
        work = current - 0.95 * outer
        lefts.append(left * jnp.sqrt(jnp.float32(total_rows)))
    return (work, jnp.stack(lefts), basis * jnp.sqrt(jnp.float32(total_cols)))


def solution(mesh):
    in_specs = (P("row", "col"), P("row", "col"), P("col", None))
    out_specs = (P("row", "col"), P(None, "row", None), P("col", None))
    return jax.shard_map(shards, mesh=mesh, in_specs=in_specs, out_specs=out_specs, check_vma=False)
```

profile of v0, /device:TPU:1, one launch (start us, length us, event | category | flops | bytes accessed | tf_op | source)
XLA Modules:
  0.0 949.6 jit_solution(10892102189534766534)
XLA Ops:
  7.2 1.1 copy-done
  8.3 6.2 fusion.2
  14.6 96.9 %all-reduce.9.cloned.1.call-done = f32[512,128]{1,0:T(8,128)} async-done(((f32[512,128]{1,0:T(8,128)}), f32[512,128]{1,0:T(8,128)}) %all-reduce.9.cloned.1.call-update) | async-done | bytes 262160 | tf_op jit(solution)/shard_map/psum | solution.py:28
  111.5 2.2 fusion.22
  114.0 100.5 %all-reduce.11.cloned.1.call-done = f32[128,128]{0,1:T(8,128)} async-done(((f32[128,128]{0,1:T(8,128)}), f32[128,128]{0,1:T(8,128)}) %all-reduce.11.cloned.1.call-update) | async-done | bytes 65552 | tf_op jit(solution)/shard_map/psum | solution.py:29
  216.3 11.7 %cholesky.74 = f32[128,128]{1,0:T(8,128)S(1)} custom-call(f32[128,128]{1,0:T(8,128)S(1)} %fusion.21), custom_call_target="Cholesky" | custom-call | tf_op jit(solution)/shard_map/jit(cholesky)/cholesky | solution.py:10
  229.4 9.8 %custom-call.10 = f32[1,128,128]{1,2,0:T(8,128)S(1)} custom-call(f32[1,128,128]{2,1,0:T(8,128)S(1)} %fusion.10), custom_call_target="InvertDiagBlocksLowerTriangular" | custom-call | tf_op jit(solution)/shard_map/jit(_solve_triangular)/triangular_solve | solution.py:11
  239.2 1.4 fusion.8
  241.3 8.3 fusion.1
  249.7 107.9 %all-reduce.13.cloned.1.call-done = f32[1664,128]{1,0:T(8,128)} async-done(((f32[1664,128]{1,0:T(8,128)}), f32[1664,128]{1,0:T(8,128)}) %all-reduce.13.cloned.1.call-update) | async-done | bytes 851984 | tf_op jit(solution)/shard_map/psum | solution.py:34
  357.6 3.5 fusion.23
  361.6 7.3 multiply_subtract_fusion.1
  369.0 82.2 %all-reduce.15.cloned.1.call-done = f32[128,128]{0,1:T(8,128)} async-done(((f32[128,128]{0,1:T(8,128)}), f32[128,128]{0,1:T(8,128)}) %all-reduce.15.cloned.1.call-update) | async-done | bytes 65552 | tf_op jit(solution)/shard_map/psum | solution.py:35
  452.9 11.7 %cholesky.85 = f32[128,128]{1,0:T(8,128)S(1)} custom-call(f32[128,128]{1,0:T(8,128)S(1)} %fusion.19), custom_call_target="Cholesky" | custom-call | tf_op jit(solution)/shard_map/jit(cholesky)/cholesky | solution.py:10
  466.0 9.8 %custom-call.11 = f32[1,128,128]{1,2,0:T(8,128)S(1)} custom-call(f32[1,128,128]{2,1,0:T(8,128)S(1)} %fusion.11), custom_call_target="InvertDiagBlocksLowerTriangular" | custom-call | tf_op jit(solution)/shard_map/jit(_solve_triangular)/triangular_solve | solution.py:11
  476.7 5.8 fusion.24
  482.6 94.2 %all-reduce.17.cloned.1.call-done = f32[512,128]{1,0:T(8,128)} async-done(((f32[512,128]{1,0:T(8,128)}), f32[512,128]{1,0:T(8,128)}) %all-reduce.17.cloned.1.call-update) | async-done | bytes 262160 | tf_op jit(solution)/shard_map/psum | solution.py:28
  576.8 2.2 fusion.25
  579.1 100.6 %all-reduce.19.cloned.1.call-done = f32[128,128]{0,1:T(8,128)} async-done(((f32[128,128]{0,1:T(8,128)}), f32[128,128]{0,1:T(8,128)}) %all-reduce.19.cloned.1.call-update) | async-done | bytes 65552 | tf_op jit(solution)/shard_map/psum | solution.py:29
  681.5 11.7 %cholesky.96 = f32[128,128]{1,0:T(8,128)S(1)} custom-call(f32[128,128]{1,0:T(8,128)S(1)} %fusion.17), custom_call_target="Cholesky" | custom-call | tf_op jit(solution)/shard_map/jit(cholesky)/cholesky | solution.py:10
  694.5 9.8 %custom-call.12 = f32[1,128,128]{1,2,0:T(8,128)S(1)} custom-call(f32[1,128,128]{2,1,0:T(8,128)S(1)} %fusion.12), custom_call_target="InvertDiagBlocksLowerTriangular" | custom-call | tf_op jit(solution)/shard_map/jit(_solve_triangular)/triangular_solve | solution.py:11
  704.3 1.4 fusion.6
  705.7 8.3 fusion.26
  714.4 1.0 copy.14
  715.4 106.6 %all-reduce.21.cloned.1.call-done = f32[1664,128]{1,0:T(8,128)} async-done(((f32[1664,128]{1,0:T(8,128)}), f32[1664,128]{1,0:T(8,128)}) %all-reduce.21.cloned.1.call-update) | async-done | bytes 851984 | tf_op jit(solution)/shard_map/psum | solution.py:34
  822.0 3.5 fusion.27
  825.6 6.4 multiply_subtract_fusion
  831.9 83.7 %all-reduce.23.cloned.1.call-done = f32[128,128]{0,1:T(8,128)} async-done(((f32[128,128]{0,1:T(8,128)}), f32[128,128]{0,1:T(8,128)}) %all-reduce.23.cloned.1.call-update) | async-done | bytes 65552 | tf_op jit(solution)/shard_map/psum | solution.py:35
  917.5 11.7 %cholesky.107 = f32[128,128]{1,0:T(8,128)S(1)} custom-call(f32[128,128]{1,0:T(8,128)S(1)} %fusion.15), custom_call_target="Cholesky" | custom-call | tf_op jit(solution)/shard_map/jit(cholesky)/cholesky | solution.py:10
  930.5 9.8 %custom-call.13 = f32[1,128,128]{1,2,0:T(8,128)S(1)} custom-call(f32[1,128,128]{2,1,0:T(8,128)S(1)} %fusion.13), custom_call_target="InvertDiagBlocksLowerTriangular" | custom-call | tf_op jit(solution)/shard_map/jit(_solve_triangular)/triangular_solve | solution.py:11
  940.3 1.0 fusion
  941.3 1.2 copy.15
  (51 shorter events, 15.5 us)
Async XLA Ops:
  7.2 1.2 copy-start
  7.2 234.1 %copy-start.1 = (bf16[512,1664]{1,0:T(8,128)(2,1)S(1)}, bf16[512,1664]{1,0:T(8,128)(2,1)}, u32[]{:S(2)}) copy-start(bf16[512,1664]{1,0:T(8,128)(2,1)} %param.9) | copy-start | bytes 5111812
  7.2 104.3 %all-reduce.9.cloned.1.call-start = ((), (), s32[]{:S(2)}) async-start(), calls=%async_computation | async-start | bytes 524288 | tf_op jit(solution)/shard_map/psum | solution.py:28
  14.5 200.0 %all-reduce.11.cloned.1.call-start = ((), (), s32[]{:S(2)}) async-start(), calls=%async_computation.1 | async-start | bytes 131072 | tf_op jit(solution)/shard_map/psum | solution.py:29
  113.8 243.8 %all-reduce.13.cloned.1.call-start = ((), (), s32[]{:S(2)}) async-start(), calls=%async_computation.2 | async-start | bytes 1703936 | tf_op jit(solution)/shard_map/psum | solution.py:34
  240.6 0.7 copy-start.4
  249.6 201.5 %all-reduce.15.cloned.1.call-start = ((), (), s32[]{:S(2)}) async-start(), calls=%async_computation.3 | async-start | bytes 131072 | tf_op jit(solution)/shard_map/psum | solution.py:35
  361.1 114.6 %copy-start.2 = (f32[1664,128]{1,0:T(8,128)S(1)}, f32[1664,128]{1,0:T(8,128)}, u32[]{:S(2)}) copy-start(f32[1664,128]{1,0:T(8,128)} %all-reduce.13.cloned.1.call-done) | copy-start | bytes 2555908
  361.2 215.6 %all-reduce.17.cloned.1.call-start = ((), (), s32[]{:S(2)}) async-start(), calls=%async_computation.4 | async-start | bytes 524288 | tf_op jit(solution)/shard_map/psum | solution.py:28
  482.5 197.1 %all-reduce.19.cloned.1.call-start = ((), (), s32[]{:S(2)}) async-start(), calls=%async_computation.5 | async-start | bytes 131072 | tf_op jit(solution)/shard_map/psum | solution.py:29
  579.0 135.3 %copy-start.5 = (f32[128,512]{1,0:T(8,128)S(1)}, f32[128,512]{1,0:T(8,128)}, u32[]{:S(2)}) copy-start(f32[128,512]{1,0:T(8,128)} %copy-done.4) | copy-start | bytes 786436
  579.0 243.0 %all-reduce.21.cloned.1.call-start = ((), (), s32[]{:S(2)}) async-start(), calls=%async_computation.6 | async-start | bytes 1703936 | tf_op jit(solution)/shard_map/psum | solution.py:34
  714.1 201.6 %all-reduce.23.cloned.1.call-start = ((), (), s32[]{:S(2)}) async-start(), calls=%async_computation.7 | async-start | bytes 131072 | tf_op jit(solution)/shard_map/psum | solution.py:35
  825.6 114.8 %copy-start.3 = (f32[1664,128]{1,0:T(8,128)S(1)}, f32[1664,128]{1,0:T(8,128)}, u32[]{:S(2)}) copy-start(f32[1664,128]{1,0:T(8,128)} %all-reduce.21.cloned.1.call-done) | copy-start | bytes 2555908
Sparse Core Ops, SparseCore 0:
  14.6 96.8 all-reduce.8
  114.5 99.9 all-reduce.10
  249.7 107.7 all-reduce.12
  361.5 89.5 all-reduce.14
  482.7 94.0 all-reduce.16
  579.6 99.9 all-reduce.18
  714.2 107.7 all-reduce.20
  826.1 89.5 all-reduce.22
where the time goes:
time: 954 us; the launch traced here: 950 us
  waiting for transfers between devices  773 us (81%)
  other arithmetic  94.9 us (10%)
  matrix products  58.5 us (6%)
  between operations  14.6 us (2%)
    psum x2, waiting for transfers between devices, shards(): right_raw = lax.psum(partial_right, 'row')  214 us
    psum x2, waiting for transfers between devices, shards(): gram_left = lax.psum(gram_of(proj), 'row')  201 us
    psum x2, waiting for transfers between devices, shards(): lax.psum(jnp.dot(current, current_basis, precision=lax.Precision.HIGHEST)...  191 us
    psum x2, waiting for transfers between devices, shards(): gram_right = lax.psum(gram_of(right_raw), 'col')  166 us
    another operation x12, other arithmetic, chol_solve(): lower = jnp.linalg.cholesky(gram)  49.6 us
    another operation x8, other arithmetic, chol_solve(): return jax.scipy.linalg.solve_triangular(lower, share.T, lower=True).T  41.9 us
  transfers between devices with their start and end apart: 8, of which 8 were waited for; matrix products, arithmetic and copies ran while one was open for 2% of the time, Pallas kernels for 0%

commit v1 on v0

v1 whole, which is shorter than its diff:
```python
import functools
import math

import jax
import jax.numpy as jnp
from jax import lax
from jax.experimental import pallas as pl
from jax.experimental.pallas import tpu as pltpu
from jax.sharding import PartitionSpec as P

RANK = 128
MESH = pl.DeviceIdType.MESH
HIGHEST = lax.Precision.HIGHEST
F32 = jnp.float32
BF16 = jnp.bfloat16
NN = (((1,), (0,)), ((), ()))
NT = (((1,), (1,)), ((), ()))
TN = (((0,), (0,)), ((), ()))


def dot(a, b, dims=NN):
    return lax.dot_general(a, b, dims, preferred_element_type=F32)


def exact(a, b, dims=NN):
    return lax.dot_general(a, b, dims, precision=HIGHEST, preferred_element_type=F32)


def split(x):
    high = x.astype(BF16)
    return high, (x - high.astype(F32)).astype(BF16)


def tiles(total, size):
    return [(i, min(size, total - i)) for i in range(0, total, size)]


def inverse_cholesky(a_ref):
    lane = lax.broadcasted_iota(jnp.int32, (8, RANK), 1)
    sub = lax.broadcasted_iota(jnp.int32, (8, RANK), 0)
    row_all = lax.broadcasted_iota(jnp.int32, (RANK, RANK), 0)
    lane_all = lax.broadcasted_iota(jnp.int32, (RANK, RANK), 1)

    def panel(k, carry):
        o = pl.multiple_of(k * 8, 8)
        v = a_ref[pl.ds(o, 8), :]
        front = pltpu.roll(v, lax.rem(RANK - o, RANK), 1)
        cols = [jnp.broadcast_to(front[:, j : j + 1], (8, RANK)) for j in range(8)]
        inside = (lane >= o) & (lane < o + 8)
        v = jnp.where(inside, jnp.where(lane == o + sub, 1.0, 0.0), v)
        for j in range(8):
            d = jnp.broadcast_to(cols[j][j : j + 1, :], (8, RANK))
            r = lax.rsqrt(d)
            r = r * (1.5 - 0.5 * d * r * r)
            m = jnp.where(sub > j, cols[j] * r, 0.0)
            scaled = jnp.broadcast_to(v[j : j + 1, :], (8, RANK)) * r
            v = jnp.where(sub == j, scaled, v - m * scaled)
            for l in range(j + 1, 8):
                e = jnp.broadcast_to(cols[l][j : j + 1, :], (8, RANK)) * r
                cols[l] = cols[l] - m * e
        behind = jnp.where(lane >= o + 8, v, 0.0)
        update = exact(behind, v, TN)
        old = a_ref[...]
        clear = (row_all >= o + 8) & (lane_all >= o) & (lane_all < o + 8)
        a_ref[...] = jnp.where(clear, 0.0, old) - update
        a_ref[pl.ds(o, 8), :] = jnp.where(lane < o + 8, v, 0.0)
        return carry

    lax.fori_loop(0, RANK // 8, panel, 0)


def kernel(
    n_col, n_z, mom_ref, grad_ref, basis_ref, mom_out, left_out, right_out,
    w, wh, wl, b2, proj, pt2, rt, rt2, left, gram,
    c_src, c_rs, c_own, c_ag, st, r_half, r_sum, r_rs, r_own, r_ag, sx, g_src, g_rs, g_own, g_ag,
    send, recv,
):
    rows, cols = mom_ref.shape
    row = lax.axis_index("row")
    me = lax.axis_index("col")
    z = row // 2
    core = lax.rem(row, 2)
    total_rows = rows * 2 * n_z
    total_cols = cols * n_col
    at_col = lambda p: (row, p)
    at_z = lambda p: (p * 2 + core, me)
    partner = (z * 2 + 1 - core, me)

    barrier = pltpu.get_barrier_semaphore()

    def greet_col(s, carry):
        pl.semaphore_signal(barrier, inc=1, device_id=at_col(lax.rem(me + s, n_col)), device_id_type=MESH)
        return carry

    def greet_z(s, carry):
        pl.semaphore_signal(barrier, inc=1, device_id=at_z(lax.rem(z + s, n_z)), device_id_type=MESH)
        return carry

    lax.fori_loop(1, n_col, greet_col, 0)
    lax.fori_loop(1, n_z, greet_z, 0)
    pl.semaphore_signal(barrier, inc=1, device_id=partner, device_id_type=MESH)
    pl.semaphore_wait(barrier, n_col + n_z - 1)

    def remote(src, dst, sem, to):
        return pltpu.make_async_remote_copy(
            src_ref=src, dst_ref=dst, send_sem=send.at[sem], recv_sem=recv.at[sem],
            device_id=to, device_id_type=MESH,
        )

    def reduce_all(n, mine, at, src, rs, own, ag, put, sem):
        def spread(s, carry):
            p = lax.rem(mine + s, n)
            remote(src.at[p], rs.at[s - 1], sem, at(p)).start()
            return carry

        lax.fori_loop(1, n, spread, 0)
        remote(rs, rs, sem, at(mine)).wait_recv()
        total = src[mine]
        for s in range(n - 1):
            total = total + rs[s]
        own[...] = total

        def gather(s, carry):
            p = lax.rem(mine + s, n)
            remote(own, ag.at[s - 1], sem + 1, at(p)).start()
            return carry

        lax.fori_loop(1, n, gather, 0)
        put(mine, total)
        remote(ag, ag, sem + 1, at(mine)).wait_recv()
        for s in range(1, n):
            put(lax.rem(mine - s + n, n), ag[s - 1])
        remote(rs, rs, sem, at(mine)).wait_send()
        remote(ag, ag, sem + 1, at(mine)).wait_send()

    def reduce_rows(sem):
        away = pl.ds(pl.multiple_of((1 - core) * n_z, n_z), n_z)
        home = pl.ds(pl.multiple_of(core * n_z, n_z), n_z)
        first = remote(st.at[away], r_half, sem, partner)
        first.start()
        first.wait()
        r_sum[...] = st[home] + r_half[...]

        def put(q, value):
            sx[core * n_z + q] = value

        reduce_all(n_z, z, at_z, r_sum, r_rs, r_own, r_ag, put, sem + 1)
        last = remote(sx.at[home], sx.at[home], sem + 3, partner)
        last.start()
        last.wait()

    def transposed_products():
        pt = proj[...].T
        h, l = split(pt)
        pt2[pl.ds(0, RANK), :] = h
        pt2[pl.ds(RANK, RANK), :] = l
        st[:, :, pl.ds(cols, RANK)] = exact(pt, pt, NT).reshape(2 * n_z, 8, RANK)
        for o, size in tiles(cols, 256):
            a = dot(pt2[...], wh[:, pl.ds(o, size)]) + dot(pt2[...], wl[:, pl.ds(o, size)])
            st[:, :, pl.ds(o, size)] = (a[:RANK] + a[RANK:]).reshape(2 * n_z, 8, size)

    def right_raw():
        gram[...] = sx[:, :, pl.ds(cols, RANK)].reshape(RANK, RANK)
        inverse_cholesky(gram)
        for o, size in tiles(cols, 256):
            value = exact(gram[...], sx[:, :, pl.ds(o, size)].reshape(RANK, size))
            rt[:, pl.ds(o, size)] = value
            h, l = split(value)
            rt2[pl.ds(0, RANK), pl.ds(o, size)] = h
            rt2[pl.ds(RANK, RANK), pl.ds(o, size)] = l
        return exact(rt[...], rt[...], NT)

    def set_left(index):
        for o, size in tiles(rows, 128):
            value = exact(proj[pl.ds(o, size), :], gram[...], NT)
            left[pl.ds(o, size), :] = value
            left_out[index, pl.ds(o, size), :] = value * F32(math.sqrt(total_rows))

    def deflate(write):
        for o, size in tiles(rows, 128):
            h, l = split(left[pl.ds(o, size), :])
            hl = jnp.concatenate([h, l], axis=1)
            lh = jnp.concatenate([l, h], axis=1)
            for p, width in tiles(cols, 256):
                outer = dot(hl, rt2[:, pl.ds(p, width)]) + dot(lh, rt2[:, pl.ds(p, width)])
                write(o, size, p, width, w[pl.ds(o, size), pl.ds(p, width)] - 0.95 * outer)

    h, l = split(basis_ref[...])
    b2[:, pl.ds(0, RANK)] = h
    b2[:, pl.ds(RANK, RANK)] = l
    per = rows // n_col

    def set_work(o, size, p, width, value):
        w[pl.ds(o, size), pl.ds(p, width)] = value
        h, l = split(value)
        wh[pl.ds(o, size), pl.ds(p, width)] = h
        wl[pl.ds(o, size), pl.ds(p, width)] = l

    for o, size in tiles(rows, 128):
        for p, width in tiles(cols, 256):
            value = mom_ref[pl.ds(o, size), pl.ds(p, width)] + grad_ref[pl.ds(o, size), pl.ds(p, width)].astype(F32)
            set_work(o, size, p, width, value)
        a = dot(wh[pl.ds(o, size), :], b2[...]) + dot(wl[pl.ds(o, size), :], b2[...])
        c_src[pl.ds(o // per, size // per), pl.ds(0, per), :] = (a[:, :RANK] + a[:, RANK:]).reshape(size // per, per, RANK)
    c_src[:, pl.ds(per, 8), :] = jnp.zeros((n_col, 8, RANK), F32)

    def put_proj(q, value):
        proj[pl.ds(pl.multiple_of(q * per, per), per), :] = value[:per]
        gram[pl.ds(pl.multiple_of(q * 8, 8), 8), :] = value[per:]

    reduce_all(n_col, me, at_col, c_src, c_rs, c_own, c_ag, put_proj, 0)
    transposed_products()
    reduce_rows(2)
    gram_part = right_raw()
    for o, size in tiles(rows, 128):
        a = dot(wh[pl.ds(o, size), :], rt2[...], NT) + dot(wl[pl.ds(o, size), :], rt2[...], NT)
        c_src[pl.ds(o // per, size // per), pl.ds(0, per), :] = (a[:, :RANK] + a[:, RANK:]).reshape(size // per, per, RANK)
    c_src[:, pl.ds(per, 8), :] = gram_part.reshape(n_col, 8, RANK)
    set_left(0)
    deflate(set_work)
    reduce_all(n_col, me, at_col, c_src, c_rs, c_own, c_ag, put_proj, 6)
    full_gram = gram[...]
    inverse_cholesky(gram)
    for o, size in tiles(rows, 128):
        value = proj[pl.ds(o, size), :] - 0.95 * exact(left[pl.ds(o, size), :], full_gram)
        proj[pl.ds(o, size), :] = exact(value, gram[...], NT)
    transposed_products()
    reduce_rows(8)
    gram_part = right_raw()
    set_left(1)

    def set_out(o, size, p, width, value):
        mom_out[pl.ds(o, size), pl.ds(p, width)] = value

    deflate(set_out)
    g_src[...] = gram_part.reshape(n_col, 8, RANK)

    def put_gram(q, value):
        gram[pl.ds(pl.multiple_of(q * 8, 8), 8), :] = value

    reduce_all(n_col, me, at_col, g_src, g_rs, g_own, g_ag, put_gram, 12)
    inverse_cholesky(gram)
    for o, size in tiles(cols, 128):
        value = exact(gram[...], rt[:, pl.ds(o, size)]) * F32(math.sqrt(total_cols))
        right_out[pl.ds(o, size), :] = value.T


def shards(momentum, grad, basis):
    rows, cols = momentum.shape
    n_col = lax.axis_size("col")
    n_z = lax.axis_size("row") // 2
    per = rows // n_col
    wide = cols + RANK
    vmem = pl.BlockSpec(memory_space=pltpu.VMEM)
    scratch = [
        ((rows, cols), F32), ((rows, cols), BF16), ((rows, cols), BF16), ((cols, 2 * RANK), BF16),
        ((rows, RANK), F32), ((2 * RANK, rows), BF16), ((RANK, cols), F32), ((2 * RANK, cols), BF16),
        ((rows, RANK), F32), ((RANK, RANK), F32),
        ((n_col, per + 8, RANK), F32), ((n_col - 1, per + 8, RANK), F32), ((per + 8, RANK), F32), ((n_col - 1, per + 8, RANK), F32),
        ((2 * n_z, 8, wide), F32), ((n_z, 8, wide), F32), ((n_z, 8, wide), F32), ((n_z - 1, 8, wide), F32),
        ((8, wide), F32), ((n_z - 1, 8, wide), F32), ((2 * n_z, 8, wide), F32),
        ((n_col, 8, RANK), F32), ((n_col - 1, 8, RANK), F32), ((8, RANK), F32), ((n_col - 1, 8, RANK), F32),
    ]
    return pl.pallas_call(
        functools.partial(kernel, n_col, n_z),
        out_shape=(
            jax.ShapeDtypeStruct((rows, cols), F32),
            jax.ShapeDtypeStruct((2, rows, RANK), F32),
            jax.ShapeDtypeStruct((cols, RANK), F32),
        ),
        in_specs=[vmem] * 3,
        out_specs=(vmem,) * 3,
        scratch_shapes=[pltpu.VMEM(s, t) for s, t in scratch]
        + [pltpu.SemaphoreType.DMA((14,)), pltpu.SemaphoreType.DMA((14,))],
        compiler_params=pltpu.CompilerParams(
            collective_id=0, has_side_effects=True, vmem_limit_bytes=56 * 1024 * 1024
        ),
    )(momentum, grad, basis)


def solution(mesh):
    in_specs = (P("row", "col"), P("row", "col"), P("col", None))
    out_specs = (P("row", "col"), P(None, "row", None), P("col", None))
    return jax.shard_map(shards, mesh=mesh, in_specs=in_specs, out_specs=out_specs, check_vma=False)
```

time: 954 us -> 163 us (0.17)
  waiting for transfers between devices: 773 us -> 0 us
  Pallas kernels: 0 us -> 155 us
  other arithmetic: 94.9 us -> 0 us
  matrix products: 58.5 us -> 0 us
  between operations: 14.6 us -> 0.66 us
    psum x8 -> x0, waiting for transfers between devices: 773 us -> none  [the longest x2 214 us: shards(): right_raw = lax.psum(partial_right, 'row')]
    pallas_call x0 -> x1, Pallas kernels: none -> 155 us  [shards(): pl.pallas_call(functools.partial(kernel, n_col, n_z), out_shape=(jax.Shap...]
    another operation x23 -> x0, other arithmetic: 91.5 us -> none  [the longest x12 49.6 us: chol_solve(): lower = jnp.linalg.cholesky(gram)]
    dot_general x10 -> x0, matrix products: 53.9 us -> none  [the longest x2 16.7 us: shards(): lax.dot_general(current, left, (((0,), (0,)), ((), ())), precision=lax.Pr...]
  transfers between devices with their start and end apart: 8 -> 0, of which waited for: 8 -> 0; matrix products, arithmetic and copies ran while one was open for 2% -> 0% of each run, Pallas kernels for 0% -> 0%
where the time goes in v1:
time: 163 us; the launch traced here: 162 us
  Pallas kernels  155 us (95%)
  local copies, waits for them, and re-layouts  5.74 us (4%)
    pallas_call x1, Pallas kernels, shards(): pl.pallas_call(functools.partial(kernel, n_col, n_z), out_shape=(jax.Shap...  155 us
    unnamed x7, local copies, waits for them, and re-layouts  5.74 us

profile of v1, /device:TPU:1, one launch (start us, length us, event | category | flops | bytes accessed | tf_op | source)
XLA Modules:
  0.0 161.6 jit_solution(7757654652937005)
XLA Ops:
  0.6 155.2 %shard_map.58 = (f32[512,1664]{1,0:T(8,128)}, f32[2,512,128]{2,1,0:T(8,128)}, f32[1664,128]{1,0:T(8,128)}) custom-call(f32[512,1664]{1,0:T(8,128)} %mom_ref.1, bf16[512,1664]{1,0:T(8,128)(2,1)} %grad_ref.1, f32[1664,128]{1,0:T(8,128)} %basis_ref.1), custom_call_target="tpu_custom_call" | custom-call | tf_op jit(solution)/shard_map/pallas_call | solution.py:264
  155.9 0.0 copy-start.1
  155.9 0.0 copy-start
  155.9 4.0 %copy.9 = f32[512,1664]{1,0:T(8,128)} copy(f32[512,1664]{1,0:T(8,128)} %get-tuple-element.6) | data formatting | bytes 6815744
  159.9 0.0 copy-done.1
  159.9 0.8 copy.10
  160.7 0.0 copy-done
  160.7 0.9 copy.11
Async XLA Ops:
  155.9 4.1 %copy-start.1 = (f32[2,512,128]{2,1,0:T(8,128)S(1)}, f32[2,512,128]{2,1,0:T(8,128)}, u32[]{:S(2)}) copy-start(f32[2,512,128]{2,1,0:T(8,128)} %get-tuple-element.7) | copy-start | bytes 1572868
  155.9 4.8 %copy-start = (f32[1664,128]{1,0:T(8,128)S(1)}, f32[1664,128]{1,0:T(8,128)}, u32[]{:S(2)}) copy-start(f32[1664,128]{1,0:T(8,128)} %get-tuple-element.8) | copy-start | bytes 2555908

commit v2 on v1

v2 whole, which is shorter than its diff:
```python
import functools
import math

import jax
import jax.numpy as jnp
from jax import lax
from jax.experimental import pallas as pl
from jax.experimental.pallas import tpu as pltpu
from jax.sharding import PartitionSpec as P

RANK = 128
TILE = 128
PIECES = 4
MESH = pl.DeviceIdType.MESH
HIGHEST = lax.Precision.HIGHEST
F32 = jnp.float32
BF16 = jnp.bfloat16
NN = (((1,), (0,)), ((), ()))
NT = (((1,), (1,)), ((), ()))
TN = (((0,), (0,)), ((), ()))


def dot(a, b, dims=NN):
    return lax.dot_general(a, b, dims, preferred_element_type=F32)


def exact(a, b, dims=NN):
    return lax.dot_general(a, b, dims, precision=HIGHEST, preferred_element_type=F32)


def split(x):
    high = x.astype(BF16)
    return high, (x - high.astype(F32)).astype(BF16)


def fold(a):
    return a[:, :RANK] + a[:, RANK:]


def tiles(total, size):
    return [(i, min(size, total - i)) for i in range(0, total, size)]


def pieces_of(cols):
    blocks = cols // 128
    edges = [blocks * i // PIECES * 128 for i in range(PIECES + 1)]
    return [(a, b - a) for a, b in zip(edges[:-1], edges[1:])]


def inverse_cholesky(a_ref, first=0, last=RANK // 8):
    lane = lax.broadcasted_iota(jnp.int32, (8, RANK), 1)
    sub = lax.broadcasted_iota(jnp.int32, (8, RANK), 0)
    row_all = lax.broadcasted_iota(jnp.int32, (RANK, RANK), 0)
    lane_all = lax.broadcasted_iota(jnp.int32, (RANK, RANK), 1)

    def panel(k, carry):
        o = pl.multiple_of(k * 8, 8)
        v = a_ref[pl.ds(o, 8), :]
        front = pltpu.roll(v, lax.rem(RANK - o, RANK), 1)
        cols = [jnp.broadcast_to(front[:, j : j + 1], (8, RANK)) for j in range(8)]
        inside = (lane >= o) & (lane < o + 8)
        v = jnp.where(inside, jnp.where(lane == o + sub, 1.0, 0.0), v)
        for j in range(8):
            d = jnp.broadcast_to(cols[j][j : j + 1, :], (8, RANK))
            r = lax.rsqrt(d)
            r = r * (1.5 - 0.5 * d * r * r)
            m = jnp.where(sub > j, cols[j] * r, 0.0)
            scaled = jnp.broadcast_to(v[j : j + 1, :], (8, RANK)) * r
            v = jnp.where(sub == j, scaled, v - m * scaled)
            for l in range(j + 1, 8):
                e = jnp.broadcast_to(cols[l][j : j + 1, :], (8, RANK)) * r
                cols[l] = cols[l] - m * e
        behind = jnp.where(lane >= o + 8, v, 0.0)
        update = exact(behind, v, TN)
        old = a_ref[...]
        clear = (row_all >= o + 8) & (lane_all >= o) & (lane_all < o + 8)
        a_ref[...] = jnp.where(clear, 0.0, old) - update
        a_ref[pl.ds(o, 8), :] = jnp.where(lane < o + 8, v, 0.0)
        return carry

    lax.fori_loop(first, last, panel, 0)


def kernel(
    n_col, n_z, mom_ref, grad_ref, basis_ref, mom_out, left_out, right_out,
    w, grads, base, wh, wl, b2, proj, pt2, rt, rt2, left, gram, full_gram, acc, left_buf, right_buf,
    c_src, c_rs, c_all, g_src, g_rs, g_all, h_src, h_rs, h_all,
    io, send, recv, *piece_refs,
):
    rows, cols = w.shape
    pieces = pieces_of(cols)
    parts = [piece_refs[i * 5 : i * 5 + 5] for i in range(PIECES)]
    row = lax.axis_index("row")
    me = lax.axis_index("col")
    z = row // 2
    core = lax.rem(row, 2)
    n_row = 2 * n_z
    total_rows = rows * n_row
    total_cols = cols * n_col
    per = rows // n_col
    at_col = lambda p: (row, p)
    at_row = lambda p: (p, me)
    at_z = lambda p: (p * 2 + core, me)
    partner = (z * 2 + 1 - core, me)
    home = pl.ds(pl.multiple_of(core * n_z, n_z), n_z)
    away = pl.ds(pl.multiple_of((1 - core) * n_z, n_z), n_z)
    row_tiles = tiles(rows, TILE)

    barrier = pltpu.get_barrier_semaphore()

    def greet_col(s, carry):
        pl.semaphore_signal(barrier, inc=1, device_id=at_col(lax.rem(me + s, n_col)), device_id_type=MESH)
        return carry

    def greet_row(s, carry):
        pl.semaphore_signal(barrier, inc=1, device_id=at_row(lax.rem(row + s, n_row)), device_id_type=MESH)
        return carry

    lax.fori_loop(1, n_col, greet_col, 0)
    lax.fori_loop(1, n_row, greet_row, 0)

    loads = [pltpu.make_async_copy(basis_ref, base, io.at[0])]
    for i, (o, size) in enumerate(row_tiles):
        loads.append(pltpu.make_async_copy(mom_ref.at[pl.ds(o, size), :], w.at[pl.ds(o, size), :], io.at[1 + 2 * i]))
        loads.append(pltpu.make_async_copy(grad_ref.at[pl.ds(o, size), :], grads.at[pl.ds(o, size), :], io.at[2 + 2 * i]))
    for load in loads:
        load.start()

    def remote(src, dst, sem, to):
        return pltpu.make_async_remote_copy(
            src_ref=src, dst_ref=dst, send_sem=send.at[sem], recv_sem=recv.at[sem],
            device_id=to, device_id_type=MESH,
        )

    def scatter(n, mine, at, src, rs, sem):
        def one(s, carry):
            p = lax.rem(mine + s, n)
            remote(src.at[p], rs.at[s - 1], sem, at(p)).start()
            return carry

        lax.fori_loop(1, n, one, 0)

    def gather(n, mine, at, src, rs, full, base_slot, sem):
        remote(rs, rs, sem, partner).wait_recv()
        total = src[mine]
        for s in range(n - 1):
            total = total + rs[s]
        slot = base_slot + mine
        full[slot] = total

        def one(s, carry):
            p = lax.rem(mine + s, n)
            remote(full.at[slot], full.at[slot], sem + 1, at(p)).start()
            return carry

        lax.fori_loop(1, n, one, 0)

    def finish(rs, sem):
        remote(rs, rs, sem + 1, partner).wait_recv()
        remote(rs, rs, sem, partner).wait_send()
        remote(rs, rs, sem + 1, partner).wait_send()

    piece_sem = lambda i: 6 + 4 * i

    def column_start(i, o, size, a):
        first, count = o // per, size // per
        c_src[pl.ds(first, count)] = a.reshape(count, per, RANK)
        for q in range(first, first + count):
            @pl.when(q != me)
            def _():
                s = lax.rem(q - me + n_col, n_col)
                remote(c_src.at[q], c_rs.at[s - 1], 0, at_col(q)).start()

    def row_sums():
        pt = proj[...].T
        h, l = split(pt)
        pt2[pl.ds(0, RANK), :] = h
        pt2[pl.ds(RANK, RANK), :] = l
        g_src[...] = exact(pt, pt, NT).reshape(n_row, 8, RANK)
        scatter(n_row, row, at_row, g_src, g_rs, 4)
        swaps = []

        def onward(i):
            st, half, total, rs, sx = parts[i]
            swaps[i].wait()
            total[...] = st[home] + half[...]
            scatter(n_z, z, at_z, total, rs, piece_sem(i) + 1)

        for i, (o, size) in enumerate(pieces):
            st, half, total, rs, sx = parts[i]
            a = dot(pt2[...], wh[:, pl.ds(o, size)]) + dot(pt2[...], wl[:, pl.ds(o, size)])
            st[...] = (a[:RANK] + a[RANK:]).reshape(n_row, 8, size)
            swap = remote(st.at[away], half, piece_sem(i), partner)
            swap.start()
            swaps.append(swap)
            if i:
                onward(i - 1)
        onward(PIECES - 1)

        def gather_piece(i):
            st, half, total, rs, sx = parts[i]
            gather(n_z, z, at_z, total, rs, sx, core * n_z, piece_sem(i) + 1)

        backs = []

        def give_back(i):
            st, half, total, rs, sx = parts[i]
            finish(rs, piece_sem(i) + 1)
            back = remote(sx.at[home], sx.at[home], piece_sem(i) + 3, partner)
            back.start()
            backs.append(back)

        gather(n_row, row, at_row, g_src, g_rs, g_all, 0, 4)
        gather_piece(0)
        gather_piece(1)
        finish(g_rs, 4)
        gram[...] = g_all[...].reshape(RANK, RANK)
        inverse_cholesky(gram, 0, 2)
        gather_piece(2)
        inverse_cholesky(gram, 2, 5)
        gather_piece(3)
        inverse_cholesky(gram, 5, 10)
        give_back(0)
        inverse_cholesky(gram, 10, 13)
        give_back(1)
        inverse_cholesky(gram, 13, 16)
        give_back(2)
        return backs, give_back

    def right_raw(backs, give_back, with_product):
        part = None
        for i, (o, size) in enumerate(pieces):
            if i == PIECES - 1:
                give_back(i)
            backs[i].wait()
            sx = parts[i][4]
            value = exact(gram[...], sx[...].reshape(RANK, size))
            rt[:, pl.ds(o, size)] = value
            h, l = split(value)
            rt2[pl.ds(0, RANK), pl.ds(o, size)] = h
            rt2[pl.ds(RANK, RANK), pl.ds(o, size)] = l
            mine = exact(value, value, NT)
            part = mine if part is None else part + mine
            if i == PIECES - 1:
                h_src[...] = part.reshape(n_col, 8, RANK)
                scatter(n_col, me, at_col, h_src, h_rs, 2)
            if with_product:
                for k, (q, height) in enumerate(row_tiles):
                    here = pl.ds(q, height)
                    wide = rt2[:, pl.ds(o, size)]
                    a = dot(wh[here, pl.ds(o, size)], wide, NT) + dot(wl[here, pl.ds(o, size)], wide, NT)
                    if i:
                        a = a + acc[here, :]
                    if i < PIECES - 1:
                        acc[here, :] = a
                    else:
                        column_start(k, q, height, fold(a))

    def set_left(index):
        for o, size in row_tiles:
            value = exact(proj[pl.ds(o, size), :], gram[...], NT)
            left[pl.ds(o, size), :] = value
            left_buf[index, pl.ds(o, size), :] = value * F32(math.sqrt(total_rows))
        copy = pltpu.make_async_copy(left_buf.at[index], left_out.at[index], io.at[9 + index])
        copy.start()
        return copy

    def deflate(o, size, again):
        h, l = split(left[pl.ds(o, size), :])
        hl = jnp.concatenate([h, l], axis=1)
        lh = jnp.concatenate([l, h], axis=1)
        for p, width in tiles(cols, 256):
            outer = dot(hl, rt2[:, pl.ds(p, width)]) + dot(lh, rt2[:, pl.ds(p, width)])
            value = w[pl.ds(o, size), pl.ds(p, width)] - 0.95 * outer
            w[pl.ds(o, size), pl.ds(p, width)] = value
            if again:
                h, l = split(value)
                wh[pl.ds(o, size), pl.ds(p, width)] = h
                wl[pl.ds(o, size), pl.ds(p, width)] = l

    loads[0].wait()
    h, l = split(base[...])
    b2[:, pl.ds(0, RANK)] = h
    b2[:, pl.ds(RANK, RANK)] = l
    for i, (o, size) in enumerate(row_tiles):
        here = pl.ds(o, size)
        loads[1 + 2 * i].wait()
        loads[2 + 2 * i].wait()
        for p, width in tiles(cols, 256):
            value = w[here, pl.ds(p, width)] + grads[here, pl.ds(p, width)].astype(F32)
            w[here, pl.ds(p, width)] = value
            h, l = split(value)
            wh[here, pl.ds(p, width)] = h
            wl[here, pl.ds(p, width)] = l
        a = fold(dot(wh[here, :], b2[...]) + dot(wl[here, :], b2[...]))
        if i == 0:
            pl.semaphore_wait(barrier, n_col + n_row - 2)
        column_start(i, o, size, a)
    gather(n_col, me, at_col, c_src, c_rs, c_all, 0, 0)
    finish(c_rs, 0)
    proj[...] = c_all[...].reshape(rows, RANK)

    right_raw(*row_sums(), True)
    left_copies = [set_left(0)]
    deflate(*row_tiles[0], True)
    gather(n_col, me, at_col, h_src, h_rs, h_all, 0, 2)
    deflate(*row_tiles[1], True)
    gather(n_col, me, at_col, c_src, c_rs, c_all, 0, 0)
    for o, size in row_tiles[2:]:
        deflate(o, size, True)
    finish(h_rs, 2)
    full_gram[...] = h_all[...].reshape(RANK, RANK)
    gram[...] = full_gram[...]
    inverse_cholesky(gram)
    finish(c_rs, 0)
    for o, size in row_tiles:
        here = pl.ds(o, size)
        value = c_all[pl.ds(o // per, size // per)].reshape(size, RANK) - 0.95 * exact(left[here, :], full_gram[...])
        proj[here, :] = exact(value, gram[...], NT)

    right_raw(*row_sums(), False)
    left_copies.append(set_left(1))
    out_copies = []

    def finish_tile(i):
        o, size = row_tiles[i]
        deflate(o, size, False)
        copy = pltpu.make_async_copy(w.at[pl.ds(o, size), :], mom_out.at[pl.ds(o, size), :], io.at[11 + i])
        copy.start()
        out_copies.append(copy)

    for i in range(2):
        finish_tile(i)
    gather(n_col, me, at_col, h_src, h_rs, h_all, 0, 2)
    for i in range(2, len(row_tiles)):
        finish_tile(i)
    finish(h_rs, 2)
    gram[...] = h_all[...].reshape(RANK, RANK)
    inverse_cholesky(gram)
    for o, size in tiles(cols, 128):
        value = exact(gram[...], rt[:, pl.ds(o, size)]) * F32(math.sqrt(total_cols))
        right_buf[pl.ds(o, size), :] = value.T
    copy = pltpu.make_async_copy(right_buf, right_out, io.at[0])
    copy.start()
    for done in left_copies + out_copies + [copy]:
        done.wait()


def shards(momentum, grad, basis):
    rows, cols = momentum.shape
    n_col = lax.axis_size("col")
    n_row = lax.axis_size("row")
    n_z = n_row // 2
    per = rows // n_col
    scratch = [
        ((rows, cols), F32), ((rows, cols), BF16), ((cols, RANK), F32), ((rows, cols), BF16), ((rows, cols), BF16),
        ((cols, 2 * RANK), BF16), ((rows, RANK), F32), ((2 * RANK, rows), BF16), ((RANK, cols), F32), ((2 * RANK, cols), BF16),
        ((rows, RANK), F32), ((RANK, RANK), F32), ((RANK, RANK), F32), ((rows, 2 * RANK), F32),
        ((2, rows, RANK), F32), ((cols, RANK), F32),
        ((n_col, per, RANK), F32), ((n_col - 1, per, RANK), F32), ((n_col, per, RANK), F32),
        ((n_row, 8, RANK), F32), ((n_row - 1, 8, RANK), F32), ((n_row, 8, RANK), F32),
        ((n_col, 8, RANK), F32), ((n_col - 1, 8, RANK), F32), ((n_col, 8, RANK), F32),
    ]
    piece_scratch = []
    for _, width in pieces_of(cols):
        for count in (n_row, n_z, n_z, n_z - 1, n_row):
            piece_scratch.append(((count, 8, width), F32))
    sems = 6 + 4 * PIECES
    return pl.pallas_call(
        functools.partial(kernel, n_col, n_z),
        out_shape=(
            jax.ShapeDtypeStruct((rows, cols), F32),
            jax.ShapeDtypeStruct((2, rows, RANK), F32),
            jax.ShapeDtypeStruct((cols, RANK), F32),
        ),
        in_specs=[pl.BlockSpec(memory_space=pl.ANY)] * 3,
        out_specs=(pl.BlockSpec(memory_space=pl.ANY),) * 3,
        scratch_shapes=[pltpu.VMEM(s, t) for s, t in scratch]
        + [pltpu.SemaphoreType.DMA((11 + rows // TILE,)), pltpu.SemaphoreType.DMA((sems,)), pltpu.SemaphoreType.DMA((sems,))]
        + [pltpu.VMEM(s, t) for s, t in piece_scratch],
        compiler_params=pltpu.CompilerParams(
            collective_id=0, has_side_effects=True, vmem_limit_bytes=56 * 1024 * 1024
        ),
    )(momentum, grad, basis)


def solution(mesh):
    in_specs = (P("row", "col"), P("row", "col"), P("col", None))
    out_specs = (P("row", "col"), P(None, "row", None), P("col", None))
    return jax.shard_map(shards, mesh=mesh, in_specs=in_specs, out_specs=out_specs, check_vma=False)
```

time: 163 us -> 129 us (0.79)
  Pallas kernels: 155 us -> 122 us
    pallas_call x1, Pallas kernels: 155 us -> 122 us  [shards(): pl.pallas_call(functools.partial(kernel, n_col, n_z), out_shape=(jax.Shap...]
where the time goes in v2:
time: 129 us
  Pallas kernels  122 us (95%)
  local copies, waits for them, and re-layouts  5.74 us (4%)
    pallas_call x1, Pallas kernels, shards(): pl.pallas_call(functools.partial(kernel, n_col, n_z), out_shape=(jax.Shap...  122 us
    unnamed x7, local copies, waits for them, and re-layouts  5.74 us

profile of v2, /device:TPU:1, one launch (start us, length us, event | category | flops | bytes accessed | tf_op | source)
XLA Modules:
  0.0 128.9 jit_solution(1774407868266758095)
XLA Ops:
  0.6 122.5 %shard_map.58 = (f32[512,1664]{1,0:T(8,128)}, f32[2,512,128]{2,1,0:T(8,128)}, f32[1664,128]{1,0:T(8,128)}) custom-call(f32[512,1664]{1,0:T(8,128)} %mom_ref.1, bf16[512,1664]{1,0:T(8,128)(2,1)} %grad_ref.1, f32[1664,128]{1,0:T(8,128)} %basis_ref.1), custom_call_target="tpu_custom_call" | custom-call | tf_op jit(solution)/shard_map/pallas_call | solution.py:369
  123.1 0.0 copy-start.1
  123.1 0.0 copy-start
  123.1 4.0 %copy.9 = f32[512,1664]{1,0:T(8,128)} copy(f32[512,1664]{1,0:T(8,128)} %get-tuple-element.6) | data formatting | bytes 6815744
  127.2 0.0 copy-done.1
  127.2 0.8 copy.10
  128.0 0.0 copy-done
  128.0 0.9 copy.11
Async XLA Ops:
  123.1 4.1 %copy-start.1 = (f32[2,512,128]{2,1,0:T(8,128)S(1)}, f32[2,512,128]{2,1,0:T(8,128)}, u32[]{:S(2)}) copy-start(f32[2,512,128]{2,1,0:T(8,128)} %get-tuple-element.7) | copy-start | bytes 1572868
  123.1 4.8 %copy-start = (f32[1664,128]{1,0:T(8,128)S(1)}, f32[1664,128]{1,0:T(8,128)}, u32[]{:S(2)}) copy-start(f32[1664,128]{1,0:T(8,128)} %get-tuple-element.8) | copy-start | bytes 2555908

commit v3 on v2

--- a/solution.py
+++ b/solution.py
@@ -10,6 +10,7 @@
 
 RANK = 128
 TILE = 128
+PANEL = 16
 PIECES = 4
 MESH = pl.DeviceIdType.MESH
 HIGHEST = lax.Precision.HIGHEST
@@ -47,43 +48,61 @@
     return [(a, b - a) for a, b in zip(edges[:-1], edges[1:])]
 
 
-def inverse_cholesky(a_ref, first=0, last=RANK // 8):
-    lane = lax.broadcasted_iota(jnp.int32, (8, RANK), 1)
-    sub = lax.broadcasted_iota(jnp.int32, (8, RANK), 0)
+def three(x):
+    high, rest = x.astype(BF16), x
+    rest = rest - high.astype(F32)
+    middle = rest.astype(BF16)
+    return high, middle, (rest - middle.astype(F32)).astype(BF16)
+
+
+def inverse_cholesky(a_ref, first=0, last=RANK // PANEL):
+    size = PANEL
+    lane = lax.broadcasted_iota(jnp.int32, (size, RANK), 1)
+    sub = lax.broadcasted_iota(jnp.int32, (size, RANK), 0)
     row_all = lax.broadcasted_iota(jnp.int32, (RANK, RANK), 0)
     lane_all = lax.broadcasted_iota(jnp.int32, (RANK, RANK), 1)
 
     def panel(k, carry):
-        o = pl.multiple_of(k * 8, 8)
-        v = a_ref[pl.ds(o, 8), :]
+        o = pl.multiple_of(k * size, size)
+        v = a_ref[pl.ds(o, size), :]
         front = pltpu.roll(v, lax.rem(RANK - o, RANK), 1)
-        cols = [jnp.broadcast_to(front[:, j : j + 1], (8, RANK)) for j in range(8)]
-        inside = (lane >= o) & (lane < o + 8)
+        cols = [jnp.broadcast_to(front[:, j : j + 1], (size, RANK)) for j in range(size)]
+        inside = (lane >= o) & (lane < o + size)
         v = jnp.where(inside, jnp.where(lane == o + sub, 1.0, 0.0), v)
-        for j in range(8):
-            d = jnp.broadcast_to(cols[j][j : j + 1, :], (8, RANK))
-            r = lax.rsqrt(d)
-            r = r * (1.5 - 0.5 * d * r * r)
-            m = jnp.where(sub > j, cols[j] * r, 0.0)
-            scaled = jnp.broadcast_to(v[j : j + 1, :], (8, RANK)) * r
-            v = jnp.where(sub == j, scaled, v - m * scaled)
-            for l in range(j + 1, 8):
-                e = jnp.broadcast_to(cols[l][j : j + 1, :], (8, RANK)) * r
-                cols[l] = cols[l] - m * e
-        behind = jnp.where(lane >= o + 8, v, 0.0)
-        update = exact(behind, v, TN)
+        pivots = []
+        for j in range(size):
+            d = cols[j][j : j + 1, :]
+            pivots.append(d)
+            d = jnp.broadcast_to(d, (8, RANK))
+            r = pl.reciprocal(d, approx=True)
+            r = r * (2.0 - d * r)
+            r = r * (2.0 - d * r)
+            m = jnp.where(sub > j, cols[j] * jnp.broadcast_to(r[:1], (size, RANK)), 0.0)
+            v = v - m * jnp.broadcast_to(v[j : j + 1, :], (size, RANK))
+            for l in range(j + 1, size):
+                cols[l] = cols[l] - m * jnp.broadcast_to(cols[l][j : j + 1, :], (size, RANK))
+        d = jnp.concatenate(pivots, axis=0)
+        r = lax.rsqrt(d)
+        v = v * (r * (1.5 - 0.5 * d * r * r))
+        h, m, l = three(jnp.where(lane >= o + size, v, 0.0))
+        high, middle, low = three(v)
+        update = dot(
+            jnp.concatenate([h, m, h, l, m, h], axis=0),
+            jnp.concatenate([high, high, middle, high, middle, low], axis=0),
+            TN,
+        )
         old = a_ref[...]
-        clear = (row_all >= o + 8) & (lane_all >= o) & (lane_all < o + 8)
+        clear = (row_all >= o + size) & (lane_all >= o) & (lane_all < o + size)
         a_ref[...] = jnp.where(clear, 0.0, old) - update
-        a_ref[pl.ds(o, 8), :] = jnp.where(lane < o + 8, v, 0.0)
+        a_ref[pl.ds(o, size), :] = jnp.where(lane < o + size, v, 0.0)
         return carry
 
     lax.fori_loop(first, last, panel, 0)
 
 
 def kernel(
-    n_col, n_z, mom_ref, grad_ref, basis_ref, mom_out, left_out, right_out,
-    w, grads, base, wh, wl, b2, proj, pt2, rt, rt2, left, gram, full_gram, acc, left_buf, right_buf,
+    n_col, n_z, mom_ref, grad_ref, basis_ref, w, left_out, right_out,
+    grads, base, wh, wl, b2, proj, pt2, rt, rt2, left, gram, full_gram, acc,
     c_src, c_rs, c_all, g_src, g_rs, g_all, h_src, h_rs, h_all,
     io, send, recv, *piece_refs,
 ):
@@ -108,16 +127,13 @@
 
     barrier = pltpu.get_barrier_semaphore()
 
-    def greet_col(s, carry):
+    def far_first(n):
+        return sorted(range(1, n), key=lambda s: -min(s, n - s))
+
+    for s in far_first(n_row):
+        pl.semaphore_signal(barrier, inc=1, device_id=at_row(lax.rem(row + s, n_row)), device_id_type=MESH)
+    for s in far_first(n_col):
         pl.semaphore_signal(barrier, inc=1, device_id=at_col(lax.rem(me + s, n_col)), device_id_type=MESH)
-        return carry
-
-    def greet_row(s, carry):
-        pl.semaphore_signal(barrier, inc=1, device_id=at_row(lax.rem(row + s, n_row)), device_id_type=MESH)
-        return carry
-
-    lax.fori_loop(1, n_col, greet_col, 0)
-    lax.fori_loop(1, n_row, greet_row, 0)
 
     loads = [pltpu.make_async_copy(basis_ref, base, io.at[0])]
     for i, (o, size) in enumerate(row_tiles):
@@ -215,15 +231,15 @@
         gather_piece(1)
         finish(g_rs, 4)
         gram[...] = g_all[...].reshape(RANK, RANK)
-        inverse_cholesky(gram, 0, 2)
+        inverse_cholesky(gram, 0, 1)
         gather_piece(2)
-        inverse_cholesky(gram, 2, 5)
+        inverse_cholesky(gram, 1, 3)
         gather_piece(3)
-        inverse_cholesky(gram, 5, 10)
+        inverse_cholesky(gram, 3, 5)
         give_back(0)
-        inverse_cholesky(gram, 10, 13)
+        inverse_cholesky(gram, 5, 7)
         give_back(1)
-        inverse_cholesky(gram, 13, 16)
+        inverse_cholesky(gram, 7, 8)
         give_back(2)
         return backs, give_back
 
@@ -260,10 +276,7 @@
         for o, size in row_tiles:
             value = exact(proj[pl.ds(o, size), :], gram[...], NT)
             left[pl.ds(o, size), :] = value
-            left_buf[index, pl.ds(o, size), :] = value * F32(math.sqrt(total_rows))
-        copy = pltpu.make_async_copy(left_buf.at[index], left_out.at[index], io.at[9 + index])
-        copy.start()
-        return copy
+            left_out[index, pl.ds(o, size), :] = value * F32(math.sqrt(total_rows))
 
     def deflate(o, size, again):
         h, l = split(left[pl.ds(o, size), :])
@@ -300,8 +313,9 @@
     finish(c_rs, 0)
     proj[...] = c_all[...].reshape(rows, RANK)
 
-    right_raw(*row_sums(), True)
-    left_copies = [set_left(0)]
+    sums = row_sums()
+    right_raw(*sums, True)
+    set_left(0)
     deflate(*row_tiles[0], True)
     gather(n_col, me, at_col, h_src, h_rs, h_all, 0, 2)
     deflate(*row_tiles[1], True)
@@ -318,32 +332,20 @@
         value = c_all[pl.ds(o // per, size // per)].reshape(size, RANK) - 0.95 * exact(left[here, :], full_gram[...])
         proj[here, :] = exact(value, gram[...], NT)
 
-    right_raw(*row_sums(), False)
-    left_copies.append(set_left(1))
-    out_copies = []
-
-    def finish_tile(i):
-        o, size = row_tiles[i]
+    sums = row_sums()
+    right_raw(*sums, False)
+    set_left(1)
+    for o, size in row_tiles[:2]:
         deflate(o, size, False)
-        copy = pltpu.make_async_copy(w.at[pl.ds(o, size), :], mom_out.at[pl.ds(o, size), :], io.at[11 + i])
-        copy.start()
-        out_copies.append(copy)
-
-    for i in range(2):
-        finish_tile(i)
     gather(n_col, me, at_col, h_src, h_rs, h_all, 0, 2)
-    for i in range(2, len(row_tiles)):
-        finish_tile(i)
+    for o, size in row_tiles[2:]:
+        deflate(o, size, False)
     finish(h_rs, 2)
     gram[...] = h_all[...].reshape(RANK, RANK)
     inverse_cholesky(gram)
     for o, size in tiles(cols, 128):
         value = exact(gram[...], rt[:, pl.ds(o, size)]) * F32(math.sqrt(total_cols))
-        right_buf[pl.ds(o, size), :] = value.T
-    copy = pltpu.make_async_copy(right_buf, right_out, io.at[0])
-    copy.start()
-    for done in left_copies + out_copies + [copy]:
-        done.wait()
+        right_out[pl.ds(o, size), :] = value.T
 
 
 def shards(momentum, grad, basis):
@@ -353,10 +355,9 @@
     n_z = n_row // 2
     per = rows // n_col
     scratch = [
-        ((rows, cols), F32), ((rows, cols), BF16), ((cols, RANK), F32), ((rows, cols), BF16), ((rows, cols), BF16),
+        ((rows, cols), BF16), ((cols, RANK), F32), ((rows, cols), BF16), ((rows, cols), BF16),
         ((cols, 2 * RANK), BF16), ((rows, RANK), F32), ((2 * RANK, rows), BF16), ((RANK, cols), F32), ((2 * RANK, cols), BF16),
         ((rows, RANK), F32), ((RANK, RANK), F32), ((RANK, RANK), F32), ((rows, 2 * RANK), F32),
-        ((2, rows, RANK), F32), ((cols, RANK), F32),
         ((n_col, per, RANK), F32), ((n_col - 1, per, RANK), F32), ((n_col, per, RANK), F32),
         ((n_row, 8, RANK), F32), ((n_row - 1, 8, RANK), F32), ((n_row, 8, RANK), F32),
         ((n_col, 8, RANK), F32), ((n_col - 1, 8, RANK), F32), ((n_col, 8, RANK), F32),
@@ -369,14 +370,14 @@
     return pl.pallas_call(
         functools.partial(kernel, n_col, n_z),
         out_shape=(
-            jax.ShapeDtypeStruct((rows, cols), F32),
-            jax.ShapeDtypeStruct((2, rows, RANK), F32),
-            jax.ShapeDtypeStruct((cols, RANK), F32),
+            pltpu.VMEM((rows, cols), F32),
+            pltpu.VMEM((2, rows, RANK), F32),
+            pltpu.VMEM((cols, RANK), F32),
         ),
         in_specs=[pl.BlockSpec(memory_space=pl.ANY)] * 3,
-        out_specs=(pl.BlockSpec(memory_space=pl.ANY),) * 3,
+        out_specs=(pl.BlockSpec(memory_space=pltpu.VMEM),) * 3,
         scratch_shapes=[pltpu.VMEM(s, t) for s, t in scratch]
-        + [pltpu.SemaphoreType.DMA((11 + rows // TILE,)), pltpu.SemaphoreType.DMA((sems,)), pltpu.SemaphoreType.DMA((sems,))]
+        + [pltpu.SemaphoreType.DMA((1 + 2 * (rows // TILE),)), pltpu.SemaphoreType.DMA((sems,)), pltpu.SemaphoreType.DMA((sems,))]
         + [pltpu.VMEM(s, t) for s, t in piece_scratch],
         compiler_params=pltpu.CompilerParams(
             collective_id=0, has_side_effects=True, vmem_limit_bytes=56 * 1024 * 1024

time: 129 us -> 115 us (0.89)
  Pallas kernels: 122 us -> 111 us
  local copies, waits for them, and re-layouts: 5.74 us -> 3.45 us
    pallas_call x1, Pallas kernels: 122 us -> 111 us  [shards(): pl.pallas_call(functools.partial(kernel, n_col, n_z), out_shape=(pltpu.VM...]
    unnamed x7 -> x3, local copies, waits for them, and re-layouts: 5.74 us -> 3.45 us
where the time goes in v3:
time: 115 us
  Pallas kernels  111 us (97%)
  local copies, waits for them, and re-layouts  3.45 us (3%)
    pallas_call x1, Pallas kernels, shards(): pl.pallas_call(functools.partial(kernel, n_col, n_z), out_shape=(pltpu.VM...  111 us
    unnamed x3, local copies, waits for them, and re-layouts  3.45 us

profile of v3, /device:TPU:1, one launch (start us, length us, event | category | flops | bytes accessed | tf_op | source)
XLA Modules:
  0.0 114.7 jit_solution(5278652976710763389)
XLA Ops:
  0.6 110.7 %shard_map.58 = (f32[512,1664]{1,0:T(8,128)S(1)}, f32[2,512,128]{2,1,0:T(8,128)S(1)}, f32[1664,128]{1,0:T(8,128)S(1)}) custom-call(f32[512,1664]{1,0:T(8,128)} %mom_ref.1, bf16[512,1664]{1,0:T(8,128)(2,1)} %grad_ref.1, f32[1664,128]{1,0:T(8,128)} %basis_ref.1), custom_call_target="tpu_custom_call" | custom-call | tf_op jit(solution)/shard_map/pallas_call | solution.py:370
  111.3 1.8 %copy.9 = f32[512,1664]{1,0:T(8,128)} copy(f32[512,1664]{1,0:T(8,128)S(1)} %get-tuple-element.3) | data formatting | bytes 6815744
  113.0 0.8 copy.10
  113.8 0.9 copy.11

commit v4 on v3

--- a/solution.py
+++ b/solution.py
@@ -12,6 +12,7 @@
 TILE = 128
 PANEL = 16
 PIECES = 4
+RELAYED = 4
 MESH = pl.DeviceIdType.MESH
 HIGHEST = lax.Precision.HIGHEST
 F32 = jnp.float32
@@ -108,7 +109,7 @@
 ):
     rows, cols = w.shape
     pieces = pieces_of(cols)
-    parts = [piece_refs[i * 5 : i * 5 + 5] for i in range(PIECES)]
+    parts = [piece_refs[i * 6 : i * 6 + 6] for i in range(PIECES)]
     row = lax.axis_index("row")
     me = lax.axis_index("col")
     z = row // 2
@@ -120,10 +121,13 @@
     at_col = lambda p: (row, p)
     at_row = lambda p: (p, me)
     at_z = lambda p: (p * 2 + core, me)
+    hop = lambda s: lax.rem(z + s, n_z)
+    assert n_z == 8
     partner = (z * 2 + 1 - core, me)
     home = pl.ds(pl.multiple_of(core * n_z, n_z), n_z)
     away = pl.ds(pl.multiple_of((1 - core) * n_z, n_z), n_z)
     row_tiles = tiles(rows, TILE)
+    order = list(range(RELAYED, PIECES)) + list(range(RELAYED))
 
     barrier = pltpu.get_barrier_semaphore()
 
@@ -171,12 +175,16 @@
 
         lax.fori_loop(1, n, one, 0)
 
+    def chunks(ref, count, sem):
+        some = ref.at[pl.ds(0, count)]
+        return remote(some, some, sem, partner)
+
     def finish(rs, sem):
         remote(rs, rs, sem + 1, partner).wait_recv()
         remote(rs, rs, sem, partner).wait_send()
         remote(rs, rs, sem + 1, partner).wait_send()
 
-    piece_sem = lambda i: 6 + 4 * i
+    piece_sem = lambda i: 6 + 6 * i
 
     def column_start(i, o, size, a):
         first, count = o // per, size // per
@@ -197,13 +205,31 @@
         swaps = []
 
         def onward(i):
-            st, half, total, rs, sx = parts[i]
+            st, half, total, rs, sx, out = parts[i]
             swaps[i].wait()
             total[...] = st[home] + half[...]
-            scatter(n_z, z, at_z, total, rs, piece_sem(i) + 1)
+            if i >= RELAYED:
+                scatter(n_z, z, at_z, total, rs, piece_sem(i) + 1)
+                return
+            sem = piece_sem(i)
+            remote(total.at[hop(5)], rs.at[4], sem + 4, at_z(hop(7))).start()
+            remote(total.at[hop(3)], rs.at[5], sem + 4, at_z(hop(1))).start()
+            remote(total.at[hop(4)], rs.at[6], sem + 4, at_z(hop(2 + 4 * core))).start()
+            remote(total.at[hop(1)], rs.at[0], sem + 1, at_z(hop(1))).start()
+            remote(total.at[hop(7)], rs.at[1], sem + 1, at_z(hop(7))).start()
+
+        def relay(i):
+            st, half, total, rs, sx, out = parts[i]
+            sem = piece_sem(i)
+            chunks(sx, 3, sem + 4).wait_recv()
+            far = rs[6]
+            out[0] = total[hop(2)] + rs[5] + jnp.where(core == 0, far, 0.0)
+            out[1] = total[hop(6)] + rs[4] + jnp.where(core == 0, 0.0, far)
+            remote(out.at[0], rs.at[2], sem + 1, at_z(hop(2))).start()
+            remote(out.at[1], rs.at[3], sem + 1, at_z(hop(6))).start()
 
         for i, (o, size) in enumerate(pieces):
-            st, half, total, rs, sx = parts[i]
+            st, half, total, rs, sx, out = parts[i]
             a = dot(pt2[...], wh[:, pl.ds(o, size)]) + dot(pt2[...], wl[:, pl.ds(o, size)])
             st[...] = (a[:RANK] + a[RANK:]).reshape(n_row, 8, size)
             swap = remote(st.at[away], half, piece_sem(i), partner)
@@ -214,40 +240,63 @@
         onward(PIECES - 1)
 
         def gather_piece(i):
-            st, half, total, rs, sx = parts[i]
-            gather(n_z, z, at_z, total, rs, sx, core * n_z, piece_sem(i) + 1)
-
-        backs = []
+            st, half, total, rs, sx, out = parts[i]
+            sem = piece_sem(i)
+            if i >= RELAYED:
+                gather(n_z, z, at_z, total, rs, sx, core * n_z, sem + 1)
+                return
+            chunks(sx, 4, sem + 1).wait_recv()
+            mine = core * n_z + z
+            sx[mine] = total[z] + ((rs[0] + rs[1]) + (rs[2] + rs[3]))
+            for s in (2, 6):
+                remote(sx.at[mine], sx.at[mine], sem + 5, at_z(hop(s))).start()
+            for s in (1, 7):
+                remote(sx.at[mine], sx.at[mine], sem + 2, at_z(hop(s))).start()
+
+        def forward(i):
+            sx = parts[i][4]
+            sem = piece_sem(i)
+            chunks(sx, 2, sem + 5).wait_recv()
+            for source, to in ((6, 1), (2, 7), (6 + 4 * core, 2 + 4 * core)):
+                slot = core * n_z + hop(source)
+                remote(sx.at[slot], sx.at[slot], sem + 2, at_z(hop(to))).start()
+
+        backs = {}
 
         def give_back(i):
-            st, half, total, rs, sx = parts[i]
-            finish(rs, piece_sem(i) + 1)
-            back = remote(sx.at[home], sx.at[home], piece_sem(i) + 3, partner)
+            st, half, total, rs, sx, out = parts[i]
+            sem = piece_sem(i)
+            if i >= RELAYED:
+                finish(rs, sem + 1)
+            else:
+                chunks(sx, 5, sem + 2).wait_recv()
+                for part, count in ((4, 3), (1, 4), (5, 2), (2, 5)):
+                    chunks(sx, count, sem + part).wait_send()
+            back = remote(sx.at[home], sx.at[home], sem + 3, partner)
             back.start()
-            backs.append(back)
+            backs[i] = back
 
         gather(n_row, row, at_row, g_src, g_rs, g_all, 0, 4)
-        gather_piece(0)
-        gather_piece(1)
+        for i in range(RELAYED):
+            relay(i)
+        for i in range(RELAYED, PIECES):
+            gather_piece(i)
+        for i in range(RELAYED):
+            gather_piece(i)
         finish(g_rs, 4)
         gram[...] = g_all[...].reshape(RANK, RANK)
-        inverse_cholesky(gram, 0, 1)
-        gather_piece(2)
-        inverse_cholesky(gram, 1, 3)
-        gather_piece(3)
-        inverse_cholesky(gram, 3, 5)
-        give_back(0)
-        inverse_cholesky(gram, 5, 7)
-        give_back(1)
-        inverse_cholesky(gram, 7, 8)
-        give_back(2)
+        inverse_cholesky(gram, 0, 5)
+        for i in range(RELAYED):
+            forward(i)
+        inverse_cholesky(gram, 5, 8)
+        for i in order[:2]:
+            give_back(i)
         return backs, give_back
 
     def right_raw(backs, give_back, with_product):
         part = None
-        for i, (o, size) in enumerate(pieces):
-            if i == PIECES - 1:
-                give_back(i)
+        for n, i in enumerate(order):
+            o, size = pieces[i]
             backs[i].wait()
             sx = parts[i][4]
             value = exact(gram[...], sx[...].reshape(RANK, size))
@@ -257,7 +306,7 @@
             rt2[pl.ds(RANK, RANK), pl.ds(o, size)] = l
             mine = exact(value, value, NT)
             part = mine if part is None else part + mine
-            if i == PIECES - 1:
+            if n == PIECES - 1:
                 h_src[...] = part.reshape(n_col, 8, RANK)
                 scatter(n_col, me, at_col, h_src, h_rs, 2)
             if with_product:
@@ -265,12 +314,14 @@
                     here = pl.ds(q, height)
                     wide = rt2[:, pl.ds(o, size)]
                     a = dot(wh[here, pl.ds(o, size)], wide, NT) + dot(wl[here, pl.ds(o, size)], wide, NT)
-                    if i:
+                    if n:
                         a = a + acc[here, :]
-                    if i < PIECES - 1:
+                    if n < PIECES - 1:
                         acc[here, :] = a
                     else:
                         column_start(k, q, height, fold(a))
+            if n + 2 < PIECES:
+                give_back(order[n + 2])
 
     def set_left(index):
         for o, size in row_tiles:
@@ -364,9 +415,9 @@
     ]
     piece_scratch = []
     for _, width in pieces_of(cols):
-        for count in (n_row, n_z, n_z, n_z - 1, n_row):
+        for count in (n_row, n_z, n_z, n_z - 1, n_row, 2):
             piece_scratch.append(((count, 8, width), F32))
-    sems = 6 + 4 * PIECES
+    sems = 6 + 6 * PIECES
     return pl.pallas_call(
         functools.partial(kernel, n_col, n_z),
         out_shape=(

time: 115 us -> 108 us (0.939)
  Pallas kernels: 111 us -> 104 us
    pallas_call x1, Pallas kernels: 111 us -> 104 us  [shards(): pl.pallas_call(functools.partial(kernel, n_col, n_z), out_shape=(pltpu.VM...]
where the time goes in v4:
time: 108 us
  Pallas kernels  104 us (96%)
  local copies, waits for them, and re-layouts  3.45 us (3%)
    pallas_call x1, Pallas kernels, shards(): pl.pallas_call(functools.partial(kernel, n_col, n_z), out_shape=(pltpu.VM...  104 us
    unnamed x3, local copies, waits for them, and re-layouts  3.45 us

profile of v4, /device:TPU:1, one launch (start us, length us, event | category | flops | bytes accessed | tf_op | source)
XLA Modules:
  0.0 108.0 jit_solution(7350070379962218791)
XLA Ops:
  0.6 104.0 %shard_map.58 = (f32[512,1664]{1,0:T(8,128)S(1)}, f32[2,512,128]{2,1,0:T(8,128)S(1)}, f32[1664,128]{1,0:T(8,128)S(1)}) custom-call(f32[512,1664]{1,0:T(8,128)} %mom_ref.1, bf16[512,1664]{1,0:T(8,128)(2,1)} %grad_ref.1, f32[1664,128]{1,0:T(8,128)} %basis_ref.1), custom_call_target="tpu_custom_call" | custom-call | tf_op jit(solution)/shard_map/pallas_call | solution.py:421
  104.6 1.8 %copy.9 = f32[512,1664]{1,0:T(8,128)} copy(f32[512,1664]{1,0:T(8,128)S(1)} %get-tuple-element.3) | data formatting | bytes 6815744
  106.4 0.8 copy.10
  107.1 0.9 copy.11

commit v5 on v4

--- a/solution.py
+++ b/solution.py
@@ -11,8 +11,7 @@
 RANK = 128
 TILE = 128
 PANEL = 16
-PIECES = 4
-RELAYED = 4
+PIECES = 3
 MESH = pl.DeviceIdType.MESH
 HIGHEST = lax.Precision.HIGHEST
 F32 = jnp.float32
@@ -56,7 +55,7 @@
     return high, middle, (rest - middle.astype(F32)).astype(BF16)
 
 
-def inverse_cholesky(a_ref, first=0, last=RANK // PANEL):
+def inverse_cholesky(a_ref, first=0, last=RANK // PANEL, unrolled=False):
     size = PANEL
     lane = lax.broadcasted_iota(jnp.int32, (size, RANK), 1)
     sub = lax.broadcasted_iota(jnp.int32, (size, RANK), 0)
@@ -64,9 +63,9 @@
     lane_all = lax.broadcasted_iota(jnp.int32, (RANK, RANK), 1)
 
     def panel(k, carry):
-        o = pl.multiple_of(k * size, size)
+        o = k * size if unrolled else pl.multiple_of(k * size, size)
         v = a_ref[pl.ds(o, size), :]
-        front = pltpu.roll(v, lax.rem(RANK - o, RANK), 1)
+        front = v[:, o : o + size] if unrolled else pltpu.roll(v, lax.rem(RANK - o, RANK), 1)
         cols = [jnp.broadcast_to(front[:, j : j + 1], (size, RANK)) for j in range(size)]
         inside = (lane >= o) & (lane < o + size)
         v = jnp.where(inside, jnp.where(lane == o + sub, 1.0, 0.0), v)
@@ -77,7 +76,6 @@
             d = jnp.broadcast_to(d, (8, RANK))
             r = pl.reciprocal(d, approx=True)
             r = r * (2.0 - d * r)
-            r = r * (2.0 - d * r)
             m = jnp.where(sub > j, cols[j] * jnp.broadcast_to(r[:1], (size, RANK)), 0.0)
             v = v - m * jnp.broadcast_to(v[j : j + 1, :], (size, RANK))
             for l in range(j + 1, size):
@@ -85,6 +83,9 @@
         d = jnp.concatenate(pivots, axis=0)
         r = lax.rsqrt(d)
         v = v * (r * (1.5 - 0.5 * d * r * r))
+        if unrolled and o + size == RANK:
+            a_ref[pl.ds(o, size), :] = v
+            return carry
         h, m, l = three(jnp.where(lane >= o + size, v, 0.0))
         high, middle, low = three(v)
         update = dot(
@@ -92,13 +93,20 @@
             jnp.concatenate([high, high, middle, high, middle, low], axis=0),
             TN,
         )
-        old = a_ref[...]
         clear = (row_all >= o + size) & (lane_all >= o) & (lane_all < o + size)
-        a_ref[...] = jnp.where(clear, 0.0, old) - update
+        value = jnp.where(clear, 0.0, a_ref[...]) - update
+        if unrolled:
+            a_ref[pl.ds(o + size, RANK - o - size), :] = value[o + size :]
+        else:
+            a_ref[...] = value
         a_ref[pl.ds(o, size), :] = jnp.where(lane < o + size, v, 0.0)
         return carry
 
-    lax.fori_loop(first, last, panel, 0)
+    if unrolled:
+        for k in range(first, last):
+            panel(k, 0)
+    else:
+        lax.fori_loop(first, last, panel, 0)
 
 
 def kernel(
@@ -118,8 +126,24 @@
     total_rows = rows * n_row
     total_cols = cols * n_col
     per = rows // n_col
-    at_col = lambda p: (row, p)
-    at_row = lambda p: (p, me)
+    wide = int(math.sqrt(n_col))
+    assert wide * wide == n_col
+    y, x = me // wide, lax.rem(me, wide)
+    near = lambda s, n: min(s, n - s)
+    col_peers = [
+        (dy * wide + dx - 1, lax.rem(y + dy, wide) * wide + lax.rem(x + dx, wide))
+        for dy, dx in sorted(
+            [(i, j) for i in range(wide) for j in range(wide) if i or j],
+            key=lambda d: -near(d[0], wide) - near(d[1], wide),
+        )
+    ]
+    row_peers = [
+        (dz * 2 + dc - 1, lax.rem(z + dz, n_z) * 2 + lax.rem(core + dc, 2))
+        for dz, dc in sorted(
+            [(i, j) for i in range(n_z) for j in range(2) if i or j], key=lambda d: -near(d[0], n_z)
+        )
+    ]
+    at = lambda group, p: (row, p) if group is col_peers else (p, me)
     at_z = lambda p: (p * 2 + core, me)
     hop = lambda s: lax.rem(z + s, n_z)
     assert n_z == 8
@@ -127,17 +151,13 @@
     home = pl.ds(pl.multiple_of(core * n_z, n_z), n_z)
     away = pl.ds(pl.multiple_of((1 - core) * n_z, n_z), n_z)
     row_tiles = tiles(rows, TILE)
-    order = list(range(RELAYED, PIECES)) + list(range(RELAYED))
+    order = list(range(PIECES))
 
     barrier = pltpu.get_barrier_semaphore()
 
-    def far_first(n):
-        return sorted(range(1, n), key=lambda s: -min(s, n - s))
-
-    for s in far_first(n_row):
-        pl.semaphore_signal(barrier, inc=1, device_id=at_row(lax.rem(row + s, n_row)), device_id_type=MESH)
-    for s in far_first(n_col):
-        pl.semaphore_signal(barrier, inc=1, device_id=at_col(lax.rem(me + s, n_col)), device_id_type=MESH)
+    for group in (row_peers, col_peers):
+        for slot, p in group:
+            pl.semaphore_signal(barrier, inc=1, device_id=at(group, p), device_id_type=MESH)
 
     loads = [pltpu.make_async_copy(basis_ref, base, io.at[0])]
     for i, (o, size) in enumerate(row_tiles):
@@ -152,28 +172,19 @@
             device_id=to, device_id_type=MESH,
         )
 
-    def scatter(n, mine, at, src, rs, sem):
-        def one(s, carry):
-            p = lax.rem(mine + s, n)
-            remote(src.at[p], rs.at[s - 1], sem, at(p)).start()
-            return carry
-
-        lax.fori_loop(1, n, one, 0)
-
-    def gather(n, mine, at, src, rs, full, base_slot, sem):
+    def scatter(group, src, rs, sem):
+        for slot, p in group:
+            remote(src.at[p], rs.at[slot], sem, at(group, p)).start()
+
+    def gather(group, src, rs, full, sem):
+        mine = me if group is col_peers else row
         remote(rs, rs, sem, partner).wait_recv()
         total = src[mine]
-        for s in range(n - 1):
+        for s in range(rs.shape[0]):
             total = total + rs[s]
-        slot = base_slot + mine
-        full[slot] = total
-
-        def one(s, carry):
-            p = lax.rem(mine + s, n)
-            remote(full.at[slot], full.at[slot], sem + 1, at(p)).start()
-            return carry
-
-        lax.fori_loop(1, n, one, 0)
+        full[mine] = total
+        for slot, p in group:
+            remote(full.at[mine], full.at[mine], sem + 1, at(group, p)).start()
 
     def chunks(ref, count, sem):
         some = ref.at[pl.ds(0, count)]
@@ -192,8 +203,9 @@
         for q in range(first, first + count):
             @pl.when(q != me)
             def _():
-                s = lax.rem(q - me + n_col, n_col)
-                remote(c_src.at[q], c_rs.at[s - 1], 0, at_col(q)).start()
+                dy = lax.rem(q // wide + wide - y, wide)
+                dx = lax.rem(q % wide + wide - x, wide)
+                remote(c_src.at[q], c_rs.at[dy * wide + dx - 1], 0, (row, q)).start()
 
     def row_sums():
         pt = proj[...].T
@@ -201,16 +213,13 @@
         pt2[pl.ds(0, RANK), :] = h
         pt2[pl.ds(RANK, RANK), :] = l
         g_src[...] = exact(pt, pt, NT).reshape(n_row, 8, RANK)
-        scatter(n_row, row, at_row, g_src, g_rs, 4)
+        scatter(row_peers, g_src, g_rs, 4)
         swaps = []
 
         def onward(i):
             st, half, total, rs, sx, out = parts[i]
             swaps[i].wait()
             total[...] = st[home] + half[...]
-            if i >= RELAYED:
-                scatter(n_z, z, at_z, total, rs, piece_sem(i) + 1)
-                return
             sem = piece_sem(i)
             remote(total.at[hop(5)], rs.at[4], sem + 4, at_z(hop(7))).start()
             remote(total.at[hop(3)], rs.at[5], sem + 4, at_z(hop(1))).start()
@@ -242,9 +251,6 @@
         def gather_piece(i):
             st, half, total, rs, sx, out = parts[i]
             sem = piece_sem(i)
-            if i >= RELAYED:
-                gather(n_z, z, at_z, total, rs, sx, core * n_z, sem + 1)
-                return
             chunks(sx, 4, sem + 1).wait_recv()
             mine = core * n_z + z
             sx[mine] = total[z] + ((rs[0] + rs[1]) + (rs[2] + rs[3]))
@@ -266,27 +272,22 @@
         def give_back(i):
             st, half, total, rs, sx, out = parts[i]
             sem = piece_sem(i)
-            if i >= RELAYED:
-                finish(rs, sem + 1)
-            else:
-                chunks(sx, 5, sem + 2).wait_recv()
-                for part, count in ((4, 3), (1, 4), (5, 2), (2, 5)):
-                    chunks(sx, count, sem + part).wait_send()
+            chunks(sx, 5, sem + 2).wait_recv()
+            for part, count in ((4, 3), (1, 4), (5, 2), (2, 5)):
+                chunks(sx, count, sem + part).wait_send()
             back = remote(sx.at[home], sx.at[home], sem + 3, partner)
             back.start()
             backs[i] = back
 
-        gather(n_row, row, at_row, g_src, g_rs, g_all, 0, 4)
-        for i in range(RELAYED):
+        gather(row_peers, g_src, g_rs, g_all, 4)
+        for i in range(PIECES):
             relay(i)
-        for i in range(RELAYED, PIECES):
-            gather_piece(i)
-        for i in range(RELAYED):
+        for i in range(PIECES):
             gather_piece(i)
         finish(g_rs, 4)
         gram[...] = g_all[...].reshape(RANK, RANK)
         inverse_cholesky(gram, 0, 5)
-        for i in range(RELAYED):
+        for i in range(PIECES):
             forward(i)
         inverse_cholesky(gram, 5, 8)
         for i in order[:2]:
@@ -308,7 +309,7 @@
             part = mine if part is None else part + mine
             if n == PIECES - 1:
                 h_src[...] = part.reshape(n_col, 8, RANK)
-                scatter(n_col, me, at_col, h_src, h_rs, 2)
+                scatter(col_peers, h_src, h_rs, 2)
             if with_product:
                 for k, (q, height) in enumerate(row_tiles):
                     here = pl.ds(q, height)
@@ -360,7 +361,7 @@
         if i == 0:
             pl.semaphore_wait(barrier, n_col + n_row - 2)
         column_start(i, o, size, a)
-    gather(n_col, me, at_col, c_src, c_rs, c_all, 0, 0)
+    gather(col_peers, c_src, c_rs, c_all, 0)
     finish(c_rs, 0)
     proj[...] = c_all[...].reshape(rows, RANK)
 
@@ -368,15 +369,15 @@
     right_raw(*sums, True)
     set_left(0)
     deflate(*row_tiles[0], True)
-    gather(n_col, me, at_col, h_src, h_rs, h_all, 0, 2)
+    gather(col_peers, h_src, h_rs, h_all, 2)
     deflate(*row_tiles[1], True)
-    gather(n_col, me, at_col, c_src, c_rs, c_all, 0, 0)
+    gather(col_peers, c_src, c_rs, c_all, 0)
     for o, size in row_tiles[2:]:
         deflate(o, size, True)
     finish(h_rs, 2)
     full_gram[...] = h_all[...].reshape(RANK, RANK)
     gram[...] = full_gram[...]
-    inverse_cholesky(gram)
+    inverse_cholesky(gram, unrolled=True)
     finish(c_rs, 0)
     for o, size in row_tiles:
         here = pl.ds(o, size)
@@ -388,12 +389,12 @@
     set_left(1)
     for o, size in row_tiles[:2]:
         deflate(o, size, False)
-    gather(n_col, me, at_col, h_src, h_rs, h_all, 0, 2)
+    gather(col_peers, h_src, h_rs, h_all, 2)
     for o, size in row_tiles[2:]:
         deflate(o, size, False)
     finish(h_rs, 2)
     gram[...] = h_all[...].reshape(RANK, RANK)
-    inverse_cholesky(gram)
+    inverse_cholesky(gram, unrolled=True)
     for o, size in tiles(cols, 128):
         value = exact(gram[...], rt[:, pl.ds(o, size)]) * F32(math.sqrt(total_cols))
         right_out[pl.ds(o, size), :] = value.T

time: 108 us -> 106 us (0.981)
  Pallas kernels: 104 us -> 102 us
    pallas_call x1, Pallas kernels: 104 us -> 102 us  [shards(): pl.pallas_call(functools.partial(kernel, n_col, n_z), out_shape=(pltpu.VM...]
where the time goes in v5:
time: 106 us
  Pallas kernels  102 us (96%)
  local copies, waits for them, and re-layouts  3.45 us (3%)
    pallas_call x1, Pallas kernels, shards(): pl.pallas_call(functools.partial(kernel, n_col, n_z), out_shape=(pltpu.VM...  102 us
    unnamed x3, local copies, waits for them, and re-layouts  3.45 us

profile of v5, /device:TPU:1, one launch (start us, length us, event | category | flops | bytes accessed | tf_op | source)
XLA Modules:
  0.0 105.7 jit_solution(7560358077788877351)
XLA Ops:
  0.6 101.6 %shard_map.58 = (f32[512,1664]{1,0:T(8,128)S(1)}, f32[2,512,128]{2,1,0:T(8,128)S(1)}, f32[1664,128]{1,0:T(8,128)S(1)}) custom-call(f32[512,1664]{1,0:T(8,128)} %mom_ref.1, bf16[512,1664]{1,0:T(8,128)(2,1)} %grad_ref.1, f32[1664,128]{1,0:T(8,128)} %basis_ref.1), custom_call_target="tpu_custom_call" | custom-call | tf_op jit(solution)/shard_map/pallas_call | solution.py:422
  102.2 1.8 %copy.9 = f32[512,1664]{1,0:T(8,128)} copy(f32[512,1664]{1,0:T(8,128)S(1)} %get-tuple-element.3) | data formatting | bytes 6815744
  104.0 0.8 copy.10
  104.8 0.9 copy.11
